TPU v7x, 32 devices: a whole 2x2x4 slice. The times are simulated.
32 devices in a mesh: parts: 2 (over y), fsdp: 16 (over z, x, core).
Axes of the slice: x: 2, y: 2, z: 4, core: 2. Of those that a mesh axis runs over, the one named last changes fastest.
Arguments:
- token_inputs_stacked: bfloat16 [8192, 8192], P(('parts', 'fsdp')), parts along dimension 0, may hold values from -6 to 6
- cotangent: bfloat16 [8192, 8192], P(('parts', 'fsdp')), parts along dimension 0, may hold values from -6 to 6
- ascending_adapter_matrix: bfloat16 [8192, 128], P('fsdp'), may hold values from -0.0625 to 0.0625
- narrow_sketch_matrix: bfloat16 [128, 16], replicated, may hold values from -0.5 to 0.5
- input_side_projection: bfloat16 [8192, 512], P('fsdp'), may hold values from -0.0625 to 0.0625
- lengths: int32 [64], P(('parts', 'fsdp')), parts along dimension 0, may hold values from 1 to 128
Outputs:
- features: float32 [64, 8192], P(('parts', 'fsdp')), parts along dimension 0
- gram: float32 [16384, 8192], P(('parts', 'fsdp')), parts along dimension 0
There are 2 independent parts, one for each index of `parts`. A program takes and returns all parts, laid end to end along the dimension named above; an argument that names none is the same for every part. Nothing has to cross between parts.
All inputs are finite; a program needn't handle non-finite values.
Results may differ from a plain program's by a relative error of at most 0.007.
Values may be sent and summed in bfloat16 or wider, within the bound.
A program may use at most 128 MiB of HBM per device.

v0:
```python
import math

import jax
import jax.numpy as jnp
from jax import lax
from jax.sharding import PartitionSpec as P


def halves(value, axis):
    high = value.astype(jnp.bfloat16)
    low = (value - high.astype(jnp.float32)).astype(jnp.bfloat16)
    return jnp.concatenate([high, low], axis=axis)


def on_device(inputs, cotangent, up, narrow, projection, lengths):
    position = lax.axis_index("fsdp")
    devices_n = lax.axis_size("fsdp")
    ex_dev = lengths.shape[0]
    seq_len = inputs.shape[0] // ex_dev
    rank = narrow.shape[1]
    f32 = jnp.float32
    folded = lax.dot_general(narrow, up, (((0,), (1,)), ((), ())), preferred_element_type=f32)
    folded = lax.all_gather(halves(folded, 0), "fsdp", axis=1, tiled=True)
    sketch = lax.dot_general(cotangent, folded, (((1,), (1,)), ((), ())), preferred_element_type=f32)
    sketch = sketch[:, :rank] + sketch[:, rank:]
    live = jnp.arange(seq_len, dtype=jnp.int32)[None, :] < lengths[:, None]
    sketch = jnp.where(live[:, :, None], sketch.reshape(ex_dev, seq_len, rank), 0.0)
    wide = inputs.reshape(ex_dev, seq_len, -1)
    mixed = jnp.einsum("esr,esd->erd", halves(sketch, 2), wide, preferred_element_type=f32)
    mixed = (mixed[:, :rank] + mixed[:, rank:]).astype(jnp.bfloat16)
    mixed = mixed.reshape(ex_dev * rank, -1)
    mixed = lax.all_to_all(mixed, "fsdp", split_axis=1, concat_axis=0, tiled=True)
    part = jnp.dot(mixed, projection, preferred_element_type=f32)
    features = lax.psum_scatter(part, "fsdp", scatter_dimension=0, tiled=True)
    features = features.reshape(ex_dev, -1) * (1.0 / math.sqrt(seq_len))
    rounded = features.astype(jnp.bfloat16)
    own_rows = rounded.shape[1] // devices_n
    all_rows = lax.all_gather(rounded, "fsdp", axis=0, tiled=True)
    own_cols = lax.dynamic_slice_in_dim(all_rows, position * own_rows, own_rows, 1)
    gram = lax.dot_general(
        own_cols, all_rows, (((0,), (0,)), ((), ())), preferred_element_type=f32
    )
    return features, gram * (1.0 / (ex_dev * devices_n))


def solution(mesh):
    rows = P(("parts", "fsdp"), None)
    in_specs = (rows, rows, P("fsdp", None), P(), P("fsdp", None), P(("parts", "fsdp")))
    return jax.shard_map(
        on_device, mesh=mesh, in_specs=in_specs, out_specs=(rows, rows), check_vma=False
    )
```

profile of v0, /device:TPU:0, one launch (start us, length us, event | category | flops | bytes accessed | tf_op | source)
XLA Modules:
  0.0 151.7 jit_solution(1453097367326386948)
XLA Ops:
  7.2 0.0 copy-start
  7.2 0.0 reduce-scatter.2.cloned.1.call-start
  7.2 0.0 copy-start.1
  7.2 0.9 iota_compare_fusion
  8.1 1.3 subtract_convert_fusion
  9.4 24.6 %all_gather.6 = bf16[32,8192]{1,0:T(8,128)(2,1)S(1)} all-gather(bf16[32,512]{1,0:T(8,128)(2,1)S(1)} %pad_maximum_fusion), channel_id=1, replica_groups=mesh['parts'=2,'fsdp'=16] {'fsdp'}, dimensions={1}, use_global_device_ids=true | all-gather | bytes 557056 | tf_op jit(solution)/shard_map/all_gather | solution.py:23
  34.0 3.5 %convolution_bitcast_fusion = f32[256,32]{0,1:T(8,128)S(1)} fusion(bf16[32,8192]{1,0:T(8,128)(2,1)S(1)} %all_gather.6, bf16[256,8192]{1,0:T(8,128)(2,1)} %param.7), kind=kOutput, calls=%fused_computation.1 | convolution fusion | flops 134217728 | bytes 4751360 | tf_op jit(solution)/shard_map/dot_general | solution.py:24
  37.6 0.0 copy-done.1
  37.6 0.7 fusion.3
  38.3 0.1 fusion
  38.4 0.2 copy.14
  38.6 0.3 copy.12
  38.9 17.1 %all_to_all.19 = bf16[32,16,512]{2,0,1:T(8,128)(2,1)S(1)} all-to-all(bf16[32,16,512]{2,0,1:T(8,128)(2,1)S(1)} %copy.12), channel_id=1, replica_groups=mesh['parts'=2,'fsdp'=16] {'fsdp'}, dimensions={1} | all-to-all | bytes 1048576 | tf_op jit(solution)/shard_map/all_to_all | solution.py:32
  56.0 0.0 copy-done
  56.0 1.4 fusion.10
  57.4 0.0 reduce-scatter.2.cloned.1.call-update
  57.4 56.9 %reduce-scatter.2.cloned.1.call-done = f32[32,512]{1,0:T(8,128)} async-done(((f32[512,512]{1,0:T(8,128)}), f32[32,512]{1,0:T(8,128)}) %reduce-scatter.2.cloned.1.call-update) | async-done | bytes 65552 | tf_op jit(solution)/shard_map/reduce_scatter | solution.py:34
  114.3 0.8 broadcast_multiply_fusion
  115.1 0.1 mul.20
  115.2 0.0 copy-start.2
  115.2 20.9 %all-gather = bf16[16,2,8192]{2,1,0:T(2,128)(2,1)S(1)} all-gather(bf16[1,2,8192]{2,1,0:T(2,128)(2,1)S(1)} %convert_bitcast_fusion), channel_id=1, replica_groups=mesh['parts'=2,'fsdp'=16] {'fsdp'}, dimensions={0}, use_global_device_ids=true | all-gather | bytes 557056 | tf_op jit(solution)/shard_map/all_gather | solution.py:38
  136.1 0.2 reshape.42
  136.3 8.5 %convolution_multiply_fusion = f32[512,8192]{1,0:T(8,128)} fusion(bf16[32,8192]{1,0:T(8,128)(2,1)S(1)} %reshape.42, s32[]{:T(128)S(6)} %select_n.8), kind=kOutput, calls=%fused_computation | convolution fusion | flops 272629760 | bytes 17334276 | tf_op jit(solution)/shard_map/dot_general | solution.py:40
  144.8 0.0 copy-done.2
  (4 shorter events, 0.1 us)
Async XLA Ops:
  7.2 48.8 %copy-start = (bf16[512,512]{1,0:T(8,128)(2,1)S(1)}, bf16[512,512]{1,0:T(8,128)(2,1)}, u32[]{:S(2)}) copy-start(bf16[512,512]{1,0:T(8,128)(2,1)} %param.10) | copy-start | bytes 1572868
  7.2 107.1 %reduce-scatter.2.cloned.1.call-start = ((), (), s32[]{:S(2)}) async-start(), calls=%async_computation.2 | async-start | bytes 1114112 | tf_op jit(solution)/shard_map/reduce_scatter | solution.py:34
  7.2 30.4 %copy-start.1 = (bf16[256,8192]{1,0:T(8,128)(2,1)S(1)}, bf16[256,8192]{1,0:T(8,128)(2,1)}, u32[]{:S(2)}) copy-start(bf16[256,8192]{1,0:T(8,128)(2,1)} %param.6) | copy-start | bytes 12582916
  115.2 29.7 %copy-start.2 = (f32[2,8192]{1,0:T(2,128)}, f32[2,8192]{1,0:T(2,128)S(1)}, u32[]{:S(2)}) copy-start(f32[2,8192]{1,0:T(2,128)S(1)} %mul.20) | copy-start | bytes 196612
Sparse Core Ops, SparseCore 0:
  57.5 56.6 reduce-scatter.1
where the time goes:
time: 152 us
  blocking collectives  62.6 us (41%)
  waiting for transfers between devices  56.9 us (37%)
  matrix products  15.5 us (10%)
  between operations  14.1 us (9%)
  other arithmetic  1.88 us (1%)
    reduce_scatter x1, waiting for transfers between devices, on_device(): features = lax.psum_scatter(part, 'fsdp', scatter_dimension=0, tiled=True)  56.9 us
    all_gather x1, blocking collectives, on_device(): folded = lax.all_gather(halves(folded, 0), 'fsdp', axis=1, tiled=True)  24.6 us
    all_gather x1, blocking collectives, on_device(): all_rows = lax.all_gather(rounded, 'fsdp', axis=0, tiled=True)  20.9 us
    all_to_all x1, blocking collectives, on_device(): lax.all_to_all(mixed, 'fsdp', split_axis=1, concat_axis=0, tiled=True)  17.1 us
    dot_general x1, matrix products, on_device(): lax.dot_general(own_cols, all_rows, (((0,), (0,)), ((), ())), preferred_e...  8.54 us
    dot_general x1, matrix products, on_device(): lax.dot_general(cotangent, folded, (((1,), (1,)), ((), ())), preferred_el...  3.54 us
  transfers between devices with their start and end apart: 1, of which 1 were waited for; matrix products, arithmetic and copies ran while one was open for 0% of the time, Pallas kernels for 0%

commit v1 on v0

v1 whole, which is shorter than its diff:
```python
import functools
import math

import jax
import jax.numpy as jnp
from jax import lax
from jax.experimental import pallas as pl
from jax.experimental.pallas import tpu as pltpu
from jax.sharding import PartitionSpec as P

BF = jnp.bfloat16
F32 = jnp.float32
NT = (((1,), (1,)), ((), ()))


def halves(value):
    high = value.astype(BF)
    low = (value - high.astype(F32)).astype(BF)
    return jnp.concatenate([high, low], axis=0)


def features_kernel(
    outer,
    len_ref, up_ref, narrow_ref, proj_ref, cot_hbm, x_hbm,
    feat_ref, all_ref,
    cot, x, folded, pin, ysend, yrecv, psend, precv,
    local_sem, bz_s, bz_r, bb_s, bb_r, bc_s, bc_r,
    fz_s, fz_r, fb_s, fb_r, fc_s, fc_r, pin_s, pin_r, y_s, y_r, p_s, p_r,
):
    me = lax.axis_index("fsdp")
    o, within = me // 4, me % 4
    b, c = within // 2, within % 2
    plane = within
    mate_b = o * 4 + (1 - b) * 2 + c
    mate_c = o * 4 + b * 2 + (1 - c)
    rank = narrow_ref.shape[1]
    ex = len_ref.shape[0]
    seq = x.shape[0] // ex
    wide = ysend.shape[2]

    def along(step):
        return lax.rem(o + step, outer) * 4 + plane

    loads = [
        pltpu.make_async_copy(cot_hbm, cot, local_sem.at[0]),
        pltpu.make_async_copy(x_hbm, x, local_sem.at[1]),
        pltpu.make_async_copy(proj_ref, pin.at[plane], local_sem.at[2]),
    ]
    for load in loads:
        load.start()

    barrier = pltpu.get_barrier_semaphore()
    for other in [along(k) for k in range(1, outer)] + [mate_b, mate_c]:
        pl.semaphore_signal(
            barrier, inc=1, device_id={"fsdp": other}, device_id_type=pl.DeviceIdType.MESH
        )

    part = lax.dot_general(
        narrow_ref[...], up_ref[...], (((0,), (1,)), ((), ())), preferred_element_type=F32
    )
    folded[me] = halves(part)
    pl.semaphore_wait(barrier, outer + 1)

    sent = []

    def send(src, dst, s_sem, r_sem, other):
        copy = pltpu.make_async_remote_copy(
            src_ref=src, dst_ref=dst, send_sem=s_sem, recv_sem=r_sem,
            device_id={"fsdp": other}, device_id_type=pl.DeviceIdType.MESH,
        )
        copy.start()
        sent.append(copy)

    def arrived(dst, sem):
        pltpu.make_async_copy(dst, dst, sem).wait()

    def gather(buf, z_s, z_r, b_s, b_r, c_s, c_r):
        for k in range(1, outer):
            send(buf.at[me], buf.at[me], z_s.at[k], z_r.at[k], along(k))
        send(buf.at[me], buf.at[me], b_s.at[0], b_r.at[0], mate_b)
        send(buf.at[me], buf.at[me], c_s.at[0], c_r.at[0], mate_c)
        for k in range(1, outer):
            slot = along(outer - k)
            arrived(buf.at[slot], z_r.at[k])
            send(buf.at[slot], buf.at[slot], b_s.at[k], b_r.at[k], mate_b)
            send(buf.at[slot], buf.at[slot], c_s.at[k], c_r.at[k], mate_c)
        for k in range(outer):
            slot = lax.rem(o + outer - k, outer) * 4 + (1 - b) * 2 + c
            arrived(buf.at[slot], b_r.at[k])
            send(buf.at[slot], buf.at[slot], c_s.at[outer + k], c_r.at[outer + k], mate_c)
        for half in range(2):
            for k in range(outer):
                arrived(buf.at[me], c_r.at[half * outer + k])

    def pin_start():
        send(proj_ref, pin.at[plane], pin_s.at[0], pin_r.at[0], mate_b)
        send(proj_ref, pin.at[plane], pin_s.at[1], pin_r.at[1], mate_c)

    pin_start()
    gather(folded, bz_s, bz_r, bb_s, bb_r, bc_s, bc_r)

    loads[0].wait()
    sketch = jnp.zeros((2 * rank, x.shape[0]), F32)
    for i in range(outer):
        block = jnp.concatenate([folded[i * 4 + j] for j in range(4)], axis=1)
        sketch += lax.dot_general(
            block, cot[:, i * wide:(i + 1) * wide], NT, preferred_element_type=F32
        )
    sketch = sketch[:rank] + sketch[rank:]
    tok = lax.broadcasted_iota(jnp.int32, (rank, seq), 1)
    mixers = [
        halves(jnp.where(tok < len_ref[e], sketch[:, e * seq:(e + 1) * seq], 0.0))
        for e in range(ex)
    ]

    loads[1].wait()
    for k in list(range(1, outer)) + [0]:
        cols = pl.ds(pl.multiple_of(lax.rem(o + k, outer) * wide, wide), wide)
        for e in range(ex):
            mixed = jnp.dot(
                mixers[e], x[e * seq:(e + 1) * seq, cols], preferred_element_type=F32
            )
            ysend[k, e * rank:(e + 1) * rank] = (mixed[:rank] + mixed[rank:]).astype(BF)
        if k:
            send(ysend.at[k], yrecv.at[k], y_s.at[k], y_r.at[k], along(k))

    loads[2].wait()
    across = (1 - b) * 2 + c
    arrived(pin.at[across], pin_r.at[0])
    send(pin.at[across], pin.at[across], pin_s.at[2], pin_r.at[2], mate_c)
    arrived(pin.at[b * 2 + 1 - c], pin_r.at[1])
    arrived(pin.at[(1 - b) * 2 + 1 - c], pin_r.at[2])

    def project(value):
        depth = wide // 4
        total = jnp.zeros((ex * rank, pin.shape[2]), F32)
        for j in range(4):
            total += jnp.dot(
                value[:, j * depth:(j + 1) * depth], pin[j], preferred_element_type=F32
            )
        return total

    total = project(ysend[0])
    for k in range(1, outer):
        arrived(yrecv.at[k], y_r.at[k])
        psend[k] = project(yrecv[k])
        send(psend.at[k], precv.at[k], p_s.at[k], p_r.at[k], along(outer - k))
    for k in range(1, outer):
        arrived(precv.at[k], p_r.at[k])
        total += precv[k]
    total = total * (1.0 / math.sqrt(seq))
    feat_ref[...] = total
    all_ref[me] = total.astype(BF)
    gather(all_ref, fz_s, fz_r, fb_s, fb_r, fc_s, fc_r)
    for copy in sent:
        copy.wait_send()


def gram_kernel(ex, all_ref, feat32_ref, gram_ref, feat_ref, rows, few, own):
    me = lax.axis_index("fsdp")
    step = pl.program_id(0)
    own_rows, kd = gram_ref.shape
    chunks, height, lanes = rows.shape
    rank = height // (all_ref.shape[0] * ex)
    total = height // rank

    def row_of(ref, r, count):
        return jnp.concatenate(
            [ref[i, pl.ds(r, count, stride=rank), :] for i in range(chunks)], axis=1
        )

    @pl.when(step == 0)
    def _():
        for i in range(chunks):
            cols = slice(i * lanes, (i + 1) * lanes)
            rows[i] = all_ref[:, :, cols].reshape(height, lanes).astype(F32)
            few[i] = feat32_ref[:, cols]
        own[...] = row_of(rows, me * own_rows // kd, total).T
        for r in range(rank):
            feat_ref[:, r * kd:(r + 1) * kd] = row_of(few, r, ex)

    left = own[pl.ds(pl.multiple_of(lax.rem(me * own_rows, kd), own_rows), own_rows), :]
    gram_ref[...] = jnp.dot(
        left.astype(BF), row_of(rows, step, total).astype(BF), preferred_element_type=F32
    ) * (1.0 / total)


def on_device(inputs, cotangent, up, narrow, projection, lengths):
    devices = lax.axis_size("fsdp")
    outer = devices // 4
    ex = lengths.shape[0]
    tokens, width = inputs.shape
    rank = narrow.shape[1]
    depth, kd = projection.shape
    rows = ex * rank
    vmem = pl.BlockSpec(memory_space=pltpu.VMEM)
    anywhere = pl.BlockSpec(memory_space=pl.ANY)
    sems = [3]
    sems += [outer, outer, outer, outer, 2 * outer, 2 * outer] * 2
    sems += [3, 3, outer, outer, outer, outer]
    feat32, everyone = pl.pallas_call(
        functools.partial(features_kernel, outer),
        out_shape=(
            jax.ShapeDtypeStruct((rows, kd), F32),
            jax.ShapeDtypeStruct((devices, rows, kd), BF),
        ),
        in_specs=[
            pl.BlockSpec(memory_space=pltpu.SMEM), vmem, vmem, anywhere, anywhere, anywhere
        ],
        out_specs=(vmem, vmem),
        scratch_shapes=[
            pltpu.VMEM((tokens, width), BF),
            pltpu.VMEM((tokens, width), BF),
            pltpu.VMEM((devices, 2 * rank, depth), BF),
            pltpu.VMEM((4, depth, kd), BF),
            pltpu.VMEM((outer, rows, 4 * depth), BF),
            pltpu.VMEM((outer, rows, 4 * depth), BF),
            pltpu.VMEM((outer, rows, kd), F32),
            pltpu.VMEM((outer, rows, kd), F32),
        ] + [pltpu.SemaphoreType.DMA((n,)) for n in sems],
        compiler_params=pltpu.CompilerParams(
            collective_id=0, has_side_effects=True, vmem_limit_bytes=48 * 1024 * 1024
        ),
        name="features",
    )(lengths, up, narrow, projection, cotangent, inputs)
    own_rows = rank * kd // devices
    total = ex * devices
    gram, features = pl.pallas_call(
        functools.partial(gram_kernel, ex),
        grid=(rank,),
        out_shape=(
            jax.ShapeDtypeStruct((own_rows, rank * kd), F32),
            jax.ShapeDtypeStruct((ex, rank * kd), F32),
        ),
        in_specs=[
            pl.BlockSpec((devices, rows, kd), lambda i: (0, 0, 0)),
            pl.BlockSpec((rows, kd), lambda i: (0, 0)),
        ],
        out_specs=(
            pl.BlockSpec((own_rows, kd), lambda i: (0, i)),
            pl.BlockSpec((ex, rank * kd), lambda i: (0, 0)),
        ),
        scratch_shapes=[
            pltpu.VMEM((kd // 128, total * rank, 128), F32),
            pltpu.VMEM((kd // 128, rows, 128), F32),
            pltpu.VMEM((kd, total), F32),
        ],
        compiler_params=pltpu.CompilerParams(vmem_limit_bytes=48 * 1024 * 1024),
        name="gram",
    )(everyone, feat32)
    return features, gram


def solution(mesh):
    rows = P(("parts", "fsdp"), None)
    in_specs = (rows, rows, P("fsdp", None), P(), P("fsdp", None), P(("parts", "fsdp")))
    return jax.shard_map(
        on_device, mesh=mesh, in_specs=in_specs, out_specs=(rows, rows), check_vma=False
    )
```

time: 152 us -> 71.6 us (0.47)
  Pallas kernels: 0 us -> 64.9 us
  blocking collectives: 62.6 us -> 0 us
  waiting for transfers between devices: 56.9 us -> 0 us
  matrix products: 15.5 us -> 0 us
  between operations: 14.1 us -> 0.64 us
  local copies, waits for them, and re-layouts: 0.73 us -> 5.59 us
  other arithmetic: 1.88 us -> 0 us
    pallas_call x0 -> x2, Pallas kernels: none -> 64.9 us  [the longest x1 54.1 us: on_device(): pl.pallas_call(functools.partial(features_kernel, outer), out_shape=(jax....]
    reduce_scatter x1 -> x0, waiting for transfers between devices: 56.9 us -> none  [on_device(): features = lax.psum_scatter(part, 'fsdp', scatter_dimension=0, tiled=True)]
    all_gather x2 -> x0, blocking collectives: 45.5 us -> none  [the longest x1 24.6 us: on_device(): folded = lax.all_gather(halves(folded, 0), 'fsdp', axis=1, tiled=True)]
    all_to_all x1 -> x0, blocking collectives: 17.1 us -> none  [on_device(): lax.all_to_all(mixed, 'fsdp', split_axis=1, concat_axis=0, tiled=True)]
    dot_general x5 -> x0, matrix products: 15.5 us -> none  [the longest x1 8.54 us: on_device(): lax.dot_general(own_cols, all_rows, (((0,), (0,)), ((), ())), preferred_e...]
    unnamed x8 -> x9, local copies, waits for them, and re-layouts: 0.38 us -> 5.59 us
  transfers between devices with their start and end apart: 1 -> 0, of which waited for: 1 -> 0; matrix products, arithmetic and copies ran while one was open for 0% -> 0% of each run, Pallas kernels for 0% -> 0%
where the time goes in v1:
time: 71.6 us; the launch traced here: 71.1 us
  Pallas kernels  64.9 us (91%)
  local copies, waits for them, and re-layouts  5.59 us (8%)
    pallas_call x1, Pallas kernels, on_device(): pl.pallas_call(functools.partial(features_kernel, outer), out_shape=(jax....  54.1 us
    pallas_call x1, Pallas kernels, on_device(): pl.pallas_call(functools.partial(gram_kernel, ex), grid=(rank,), out_shap...  10.8 us
    unnamed x9, local copies, waits for them, and re-layouts  5.59 us

profile of v1, /device:TPU:0, one launch (start us, length us, event | category | flops | bytes accessed | tf_op | source)
XLA Modules:
  0.0 71.1 jit_solution(1874085680510466947)
XLA Ops:
  0.6 0.8 %copy.8.narrow_ref = bf16[128,16]{1,0:T(8,128)(2,1)S(1)} copy(bf16[128,16]{0,1:T(8,128)(2,1)} %param.9) | data formatting | bytes 8192 | tf_op args[3]
  1.4 0.0 copy-start
  1.4 2.2 %copy-done = bf16[256,8192]{1,0:T(8,128)(2,1)S(1)} copy-done((bf16[256,8192]{1,0:T(8,128)(2,1)S(1)}, bf16[256,8192]{1,0:T(8,128)(2,1)}, u32[]{:S(2)}) %copy-start) | copy-done | bytes 4194328
  3.6 0.0 copy-start.1
  3.6 1.0 %copy-done.1 = bf16[512,512]{1,0:T(8,128)(2,1)S(1)} copy-done((bf16[512,512]{1,0:T(8,128)(2,1)S(1)}, bf16[512,512]{1,0:T(8,128)(2,1)}, u32[]{:S(2)}) %copy-start.1) | copy-done | bytes 524312
  4.7 0.0 copy-start.2
  4.7 0.9 %copy-done.2 = bf16[512,128]{1,0:T(8,128)(2,1)S(1)} copy-done((bf16[512,128]{1,0:T(8,128)(2,1)S(1)}, bf16[512,128]{1,0:T(8,128)(2,1)}, u32[]{:S(2)}) %copy-start.2) | copy-done | bytes 131096
  5.6 0.0 copy-start.3
  5.6 0.7 copy-done.3
  6.2 54.1 %features.1 = (f32[32,512]{1,0:T(8,128)S(1)}, bf16[16,32,512]{2,1,0:T(8,128)(2,1)S(1)}) custom-call(s32[2]{0:T(128)S(1)} %copy-done.3, bf16[512,128]{1,0:T(8,128)(2,1)S(1)} %copy-done.2, bf16[128,16]{1,0:T(8,128)(2,1)S(1)} %copy.8.narrow_ref, bf16[512,512]{1,0:T(8,128)(2,1)S(1)} %copy-done.1, bf16[256,8192]{1,0:T(8,128)(2,1)S(1)} %copy-done, ...), custom_call_target="tpu_custom_call" | custom-call | tf_op jit(solution)/shard_map/features/pallas_call | solution.py:201
  60.3 10.8 %gram.1 = (f32[512,8192]{1,0:T(8,128)}, f32[2,8192]{1,0:T(2,128)}) custom-call(bf16[16,32,512]{2,1,0:T(8,128)(2,1)S(1)} %get-tuple-element.6.all_ref, f32[32,512]{1,0:T(8,128)S(1)} %get-tuple-element.7.feat32_ref), custom_call_target="tpu_custom_call" | custom-call | tf_op jit(solution)/shard_map/gram/pallas_call | solution.py:228
Async XLA Ops:
  1.4 2.2 %copy-start = (bf16[256,8192]{1,0:T(8,128)(2,1)S(1)}, bf16[256,8192]{1,0:T(8,128)(2,1)}, u32[]{:S(2)}) copy-start(bf16[256,8192]{1,0:T(8,128)(2,1)} %cot_hbm.1) | copy-start | bytes 12582916
  3.6 1.0 %copy-start.1 = (bf16[512,512]{1,0:T(8,128)(2,1)S(1)}, bf16[512,512]{1,0:T(8,128)(2,1)}, u32[]{:S(2)}) copy-start(bf16[512,512]{1,0:T(8,128)(2,1)} %proj_ref.1) | copy-start | bytes 1572868
  4.7 0.9 %copy-start.2 = (bf16[512,128]{1,0:T(8,128)(2,1)S(1)}, bf16[512,128]{1,0:T(8,128)(2,1)}, u32[]{:S(2)}) copy-start(bf16[512,128]{1,0:T(8,128)(2,1)} %up_ref.1) | copy-start | bytes 393220
  5.6 0.7 copy-start.3

commit v2 on v1

v2 whole, which is shorter than its diff:
```python
import functools
import math

import jax
import jax.numpy as jnp
from jax import lax
from jax.experimental import pallas as pl
from jax.experimental.pallas import tpu as pltpu
from jax.sharding import PartitionSpec as P

BF = jnp.bfloat16
F32 = jnp.float32
NT = (((1,), (1,)), ((), ()))


def halves(value):
    high = value.astype(BF)
    low = (value - high.astype(F32)).astype(BF)
    return jnp.concatenate([high, low], axis=0)


def features_kernel(
    outer,
    len_hbm, up_hbm, narrow_hbm, proj_ref, cot_hbm, x_hbm,
    feat_ref, all_ref,
    len_ref, up_ref, narrow_ref, cot, x, folded, pin, ysend, yrecv, psend, precv,
    local_sem, bz_s, bz_r, bb_s, bb_r, bc_s, bc_r,
    fz_s, fz_r, fb_s, fb_r, fc_s, fc_r, pin_s, pin_r, y_s, y_r, p_s, p_r,
):
    me = lax.axis_index("fsdp")
    o, within = me // 4, me % 4
    b, c = within // 2, within % 2
    plane = within
    mate_b = o * 4 + (1 - b) * 2 + c
    mate_c = o * 4 + b * 2 + (1 - c)
    rank = narrow_ref.shape[0]
    ex = len_ref.shape[0]
    seq = x.shape[0] // ex
    wide = ysend.shape[2]

    def along(step):
        return lax.rem(o + step, outer) * 4 + plane

    early = [
        pltpu.make_async_copy(up_hbm, up_ref, local_sem.at[3]),
        pltpu.make_async_copy(narrow_hbm, narrow_ref, local_sem.at[4]),
        pltpu.make_async_copy(len_hbm, len_ref, local_sem.at[5]),
    ]
    loads = [
        pltpu.make_async_copy(cot_hbm, cot, local_sem.at[0]),
        pltpu.make_async_copy(x_hbm, x, local_sem.at[1]),
        pltpu.make_async_copy(proj_ref, pin.at[plane], local_sem.at[2]),
    ]
    for load in early + loads:
        load.start()

    barrier = pltpu.get_barrier_semaphore()
    for other in [along(k) for k in range(1, outer)] + [mate_b, mate_c]:
        pl.semaphore_signal(
            barrier, inc=1, device_id={"fsdp": other}, device_id_type=pl.DeviceIdType.MESH
        )

    for load in early:
        load.wait()
    part = lax.dot_general(narrow_ref[...], up_ref[...], NT, preferred_element_type=F32)
    folded[me] = halves(part)
    pl.semaphore_wait(barrier, outer + 1)

    sent = []

    def send(src, dst, s_sem, r_sem, other):
        copy = pltpu.make_async_remote_copy(
            src_ref=src, dst_ref=dst, send_sem=s_sem, recv_sem=r_sem,
            device_id={"fsdp": other}, device_id_type=pl.DeviceIdType.MESH,
        )
        copy.start()
        sent.append(copy)

    def arrived(dst, sem):
        pltpu.make_async_copy(dst, dst, sem).wait()

    def gather(buf, z_s, z_r, b_s, b_r, c_s, c_r):
        for k in range(1, outer):
            send(buf.at[me], buf.at[me], z_s.at[k], z_r.at[k], along(k))
        send(buf.at[me], buf.at[me], b_s.at[0], b_r.at[0], mate_b)
        send(buf.at[me], buf.at[me], c_s.at[0], c_r.at[0], mate_c)
        for k in range(1, outer):
            slot = along(outer - k)
            arrived(buf.at[slot], z_r.at[k])
            send(buf.at[slot], buf.at[slot], b_s.at[k], b_r.at[k], mate_b)
            send(buf.at[slot], buf.at[slot], c_s.at[k], c_r.at[k], mate_c)
        for k in range(outer):
            slot = lax.rem(o + outer - k, outer) * 4 + (1 - b) * 2 + c
            arrived(buf.at[slot], b_r.at[k])
            send(buf.at[slot], buf.at[slot], c_s.at[outer + k], c_r.at[outer + k], mate_c)
        for half in range(2):
            for k in range(outer):
                arrived(buf.at[me], c_r.at[half * outer + k])

    depth = wide // 4
    pieces = 4
    high = depth // pieces

    def piece(slot, i):
        return pin.at[slot, pl.ds(i * high, high)]

    def pin_start(i):
        source = proj_ref.at[pl.ds(i * high, high)]
        send(source, piece(plane, i), pin_s.at[0, i], pin_r.at[0, i], mate_b)

    pin_start(0)
    gather(folded, bz_s, bz_r, bb_s, bb_r, bc_s, bc_r)
    for i in range(1, pieces):
        pin_start(i)
    send(proj_ref, pin.at[plane], pin_s.at[1, 0], pin_r.at[1, 0], mate_c)

    loads[0].wait()
    sketch = jnp.zeros((2 * rank, x.shape[0]), F32)
    for i in range(outer):
        block = jnp.concatenate([folded[i * 4 + j] for j in range(4)], axis=1)
        sketch += lax.dot_general(
            block, cot[:, i * wide:(i + 1) * wide], NT, preferred_element_type=F32
        )
    sketch = sketch[:rank] + sketch[rank:]
    tok = lax.broadcasted_iota(jnp.int32, (rank, seq), 1)
    mixers = [
        halves(jnp.where(tok < len_ref[e], sketch[:, e * seq:(e + 1) * seq], 0.0))
        for e in range(ex)
    ]

    loads[1].wait()
    for k in list(range(1, outer)) + [0]:
        cols = pl.ds(pl.multiple_of(lax.rem(o + k, outer) * wide, wide), wide)
        for e in range(ex):
            mixed = jnp.dot(
                mixers[e], x[e * seq:(e + 1) * seq, cols], preferred_element_type=F32
            )
            mixed = (mixed[:rank] + mixed[rank:]).astype(BF)
            if k:
                ysend[k, e * rank:(e + 1) * rank] = mixed
            else:
                yrecv[k, e * rank:(e + 1) * rank] = mixed
        if k:
            send(ysend.at[k], yrecv.at[k], y_s.at[k], y_r.at[k], along(k))

    loads[2].wait()
    across = (1 - b) * 2 + c
    for i in range(pieces):
        arrived(piece(across, i), pin_r.at[0, i])
        send(piece(across, i), piece(across, i), pin_s.at[2, i], pin_r.at[2, i], mate_c)
    arrived(pin.at[b * 2 + 1 - c], pin_r.at[1, 0])
    for i in range(pieces):
        arrived(piece((1 - b) * 2 + 1 - c, i), pin_r.at[2, i])
    for k in range(1, outer):
        arrived(yrecv.at[k], y_r.at[k])

    mixed = yrecv[...].reshape(outer * ex * rank, wide)
    parts = jnp.zeros((outer * ex * rank, pin.shape[2]), F32)
    for j in range(4):
        parts += jnp.dot(
            mixed[:, j * depth:(j + 1) * depth], pin[j], preferred_element_type=F32
        )
    for k in range(1, outer):
        psend[k] = parts[k * ex * rank:(k + 1) * ex * rank].astype(BF)
        send(psend.at[k], precv.at[k], p_s.at[k], p_r.at[k], along(outer - k))
    total = parts[:ex * rank]
    for k in range(1, outer):
        arrived(precv.at[k], p_r.at[k])
        total += precv[k].astype(F32)
    total = total * (1.0 / math.sqrt(seq))
    feat_ref[...] = total
    all_ref[me] = total.astype(BF)
    gather(all_ref, fz_s, fz_r, fb_s, fb_r, fc_s, fc_r)
    for copy in sent:
        copy.wait_send()


def gram_kernel(ex, all_ref, feat32_ref, gram_hbm, feat_ref, rows, few, own, tiles, sems):
    me = lax.axis_index("fsdp")
    _, own_rows, kd = tiles.shape
    chunks, height, lanes = rows.shape
    rank = height // (all_ref.shape[0] * ex)
    total = height // rank

    def row_of(ref, r, count):
        return jnp.concatenate(
            [ref[i, pl.ds(r, count, stride=rank), :] for i in range(chunks)], axis=1
        )

    for i in range(chunks):
        cols = slice(i * lanes, (i + 1) * lanes)
        rows[i] = all_ref[:, :, cols].reshape(height, lanes).astype(F32)
        few[i] = feat32_ref[:, cols]
    own[...] = row_of(rows, me * own_rows // kd, total).T
    left = own[pl.ds(pl.multiple_of(lax.rem(me * own_rows, kd), own_rows), own_rows), :]
    left = left.astype(BF)
    writes = []
    for r in range(rank):
        tiles[r] = jnp.dot(
            left, row_of(rows, r, total).astype(BF), preferred_element_type=F32
        ) * (1.0 / total)
        write = pltpu.make_async_copy(
            tiles.at[r], gram_hbm.at[:, r * kd:(r + 1) * kd], sems.at[r]
        )
        write.start()
        writes.append(write)
    for r in range(rank):
        feat_ref[:, r * kd:(r + 1) * kd] = row_of(few, r, ex)
    for write in writes:
        write.wait()


def on_device(inputs, cotangent, up, narrow, projection, lengths):
    devices = lax.axis_size("fsdp")
    outer = devices // 4
    ex = lengths.shape[0]
    tokens, width = inputs.shape
    rank = narrow.shape[1]
    depth, kd = projection.shape
    rows = ex * rank
    vmem = pl.BlockSpec(memory_space=pltpu.VMEM)
    hbm = pl.BlockSpec(memory_space=pltpu.HBM)
    sems = [6]
    sems += [outer, outer, outer, outer, 2 * outer, 2 * outer] * 2
    sems += [(3, 4), (3, 4), outer, outer, outer, outer]
    feat32, everyone = pl.pallas_call(
        functools.partial(features_kernel, outer),
        out_shape=(
            jax.ShapeDtypeStruct((rows, kd), F32),
            jax.ShapeDtypeStruct((devices, rows, kd), BF),
        ),
        in_specs=[hbm] * 6,
        out_specs=(vmem, vmem),
        scratch_shapes=[
            pltpu.SMEM((ex,), jnp.int32),
            pltpu.VMEM((depth, up.shape[1]), BF),
            pltpu.VMEM((rank, up.shape[1]), BF),
            pltpu.VMEM((tokens, width), BF),
            pltpu.VMEM((tokens, width), BF),
            pltpu.VMEM((devices, 2 * rank, depth), BF),
            pltpu.VMEM((4, depth, kd), BF),
            pltpu.VMEM((outer, rows, 4 * depth), BF),
            pltpu.VMEM((outer, rows, 4 * depth), BF),
            pltpu.VMEM((outer, rows, kd), BF),
            pltpu.VMEM((outer, rows, kd), BF),
        ] + [pltpu.SemaphoreType.DMA(n if isinstance(n, tuple) else (n,)) for n in sems],
        compiler_params=pltpu.CompilerParams(
            collective_id=0, has_side_effects=True, vmem_limit_bytes=63 * 1024 * 1024
        ),
        name="features",
    )(lengths, up, narrow.T, projection, cotangent, inputs)
    own_rows = rank * kd // devices
    total = ex * devices
    gram, features = pl.pallas_call(
        functools.partial(gram_kernel, ex),
        out_shape=(
            jax.ShapeDtypeStruct((own_rows, rank * kd), F32),
            jax.ShapeDtypeStruct((ex, rank * kd), F32),
        ),
        in_specs=[vmem, vmem],
        out_specs=(hbm, vmem),
        scratch_shapes=[
            pltpu.VMEM((kd // 128, total * rank, 128), F32),
            pltpu.VMEM((kd // 128, rows, 128), F32),
            pltpu.VMEM((kd, total), F32),
            pltpu.VMEM((rank, own_rows, kd), F32),
            pltpu.SemaphoreType.DMA((rank,)),
        ],
        compiler_params=pltpu.CompilerParams(vmem_limit_bytes=63 * 1024 * 1024),
        name="gram",
    )(everyone, feat32)
    return features, gram


def solution(mesh):
    rows = P(("parts", "fsdp"), None)
    in_specs = (rows, rows, P("fsdp", None), P(), P("fsdp", None), P(("parts", "fsdp")))
    return jax.shard_map(
        on_device, mesh=mesh, in_specs=in_specs, out_specs=(rows, rows), check_vma=False
    )
```

time: 71.6 us -> 51.8 us (0.72)
  Pallas kernels: 64.9 us -> 51 us
  local copies, waits for them, and re-layouts: 5.59 us -> 0 us
    pallas_call x1, Pallas kernels: 54.1 us -> 42.8 us  [on_device(): pl.pallas_call(functools.partial(features_kernel, outer), out_shape=(jax....]
    unnamed x9 -> x0, local copies, waits for them, and re-layouts: 5.59 us -> none
    pallas_call x1, Pallas kernels: 10.8 us -> 8.14 us  [on_device(): pl.pallas_call(functools.partial(gram_kernel, ex), out_shape=(jax.ShapeDt...]
where the time goes in v2:
time: 51.8 us; the launch traced here: 51.6 us
  Pallas kernels  51 us (98%)
  between operations  0.64 us (1%)
    pallas_call x1, Pallas kernels, on_device(): pl.pallas_call(functools.partial(features_kernel, outer), out_shape=(jax....  42.8 us
    pallas_call x1, Pallas kernels, on_device(): pl.pallas_call(functools.partial(gram_kernel, ex), out_shape=(jax.ShapeDt...  8.14 us

profile of v2, /device:TPU:0, one launch (start us, length us, event | category | flops | bytes accessed | tf_op | source)
XLA Modules:
  0.0 51.6 jit_solution(2794741255497507949)
XLA Ops:
  0.6 42.8 %features.1 = (f32[32,512]{1,0:T(8,128)}, bf16[16,32,512]{2,1,0:T(8,128)(2,1)}) custom-call(s32[2]{0:T(128)} %len_hbm.1, bf16[512,128]{1,0:T(8,128)(2,1)} %up_hbm.1, bf16[16,128]{1,0:T(8,128)(2,1)} %bitcast.1, bf16[512,512]{1,0:T(8,128)(2,1)} %proj_ref.1, bf16[256,8192]{1,0:T(8,128)(2,1)} %cot_hbm.1, bf16[256,8192]{1,0:T(8,128)(2,1)} %x_hbm.1), custom_call_target="tpu_custom_call" | custom-call | tf_op jit(solution)/shard_map/features/pallas_call | solution.py:226
  43.5 8.1 %gram.1 = (f32[512,8192]{1,0:T(8,128)}, f32[2,8192]{1,0:T(2,128)}) custom-call(bf16[16,32,512]{2,1,0:T(8,128)(2,1)} %get-tuple-element.6.all_ref, f32[32,512]{1,0:T(8,128)} %get-tuple-element.7.feat32_ref), custom_call_target="tpu_custom_call" | custom-call | tf_op jit(solution)/shard_map/gram/pallas_call | solution.py:254

commit v3 on v2

--- a/solution.py
+++ b/solution.py
@@ -67,6 +67,7 @@
     pl.semaphore_wait(barrier, outer + 1)
 
     sent = []
+    order = sorted(range(1, outer), key=lambda k: abs(k - outer // 2))
 
     def send(src, dst, s_sem, r_sem, other):
         copy = pltpu.make_async_remote_copy(
@@ -84,7 +85,7 @@
             send(buf.at[me], buf.at[me], z_s.at[k], z_r.at[k], along(k))
         send(buf.at[me], buf.at[me], b_s.at[0], b_r.at[0], mate_b)
         send(buf.at[me], buf.at[me], c_s.at[0], c_r.at[0], mate_c)
-        for k in range(1, outer):
+        for k in reversed(order):
             slot = along(outer - k)
             arrived(buf.at[slot], z_r.at[k])
             send(buf.at[slot], buf.at[slot], b_s.at[k], b_r.at[k], mate_b)
@@ -129,7 +130,7 @@
     ]
 
     loads[1].wait()
-    for k in list(range(1, outer)) + [0]:
+    for k in order + [0]:
         cols = pl.ds(pl.multiple_of(lax.rem(o + k, outer) * wide, wide), wide)
         for e in range(ex):
             mixed = jnp.dot(
@@ -155,17 +156,27 @@
         arrived(yrecv.at[k], y_r.at[k])
 
     mixed = yrecv[...].reshape(outer * ex * rank, wide)
-    parts = jnp.zeros((outer * ex * rank, pin.shape[2]), F32)
-    for j in range(4):
-        parts += jnp.dot(
-            mixed[:, j * depth:(j + 1) * depth], pin[j], preferred_element_type=F32
-        )
+    split = pin.shape[2] // 2
+    own = []
+    for h in range(2):
+        cols = slice(h * split, (h + 1) * split)
+        parts = jnp.zeros((outer * ex * rank, split), F32)
+        for j in range(4):
+            parts += jnp.dot(
+                mixed[:, j * depth:(j + 1) * depth], pin[j, :, cols],
+                preferred_element_type=F32,
+            )
+        for k in order:
+            psend[k, :, cols] = parts[k * ex * rank:(k + 1) * ex * rank].astype(BF)
+            send(
+                psend.at[k, :, cols], precv.at[k, :, cols],
+                p_s.at[h, k], p_r.at[h, k], along(outer - k),
+            )
+        own.append(parts[:ex * rank])
+    total = jnp.concatenate(own, axis=1)
     for k in range(1, outer):
-        psend[k] = parts[k * ex * rank:(k + 1) * ex * rank].astype(BF)
-        send(psend.at[k], precv.at[k], p_s.at[k], p_r.at[k], along(outer - k))
-    total = parts[:ex * rank]
-    for k in range(1, outer):
-        arrived(precv.at[k], p_r.at[k])
+        for h in range(2):
+            arrived(precv.at[k, :, h * split:(h + 1) * split], p_r.at[h, k])
         total += precv[k].astype(F32)
     total = total * (1.0 / math.sqrt(seq))
     feat_ref[...] = total
@@ -222,7 +233,7 @@
     hbm = pl.BlockSpec(memory_space=pltpu.HBM)
     sems = [6]
     sems += [outer, outer, outer, outer, 2 * outer, 2 * outer] * 2
-    sems += [(3, 4), (3, 4), outer, outer, outer, outer]
+    sems += [(3, 4), (3, 4), outer, outer, (2, outer), (2, outer)]
     feat32, everyone = pl.pallas_call(
         functools.partial(features_kernel, outer),
         out_shape=(

time: 51.8 us -> 51.8 us (level)
  no operation moved by 1% of the time
where the time goes in v3:
time: 51.8 us; the launch traced here: 51.6 us
  Pallas kernels  51 us (98%)
  between operations  0.64 us (1%)
    pallas_call x1, Pallas kernels, on_device(): pl.pallas_call(functools.partial(features_kernel, outer), out_shape=(jax....  42.8 us
    pallas_call x1, Pallas kernels, on_device(): pl.pallas_call(functools.partial(gram_kernel, ex), out_shape=(jax.ShapeDt...  8.14 us

profile of v3, /device:TPU:0, one launch (start us, length us, event | category | flops | bytes accessed | tf_op | source)
XLA Modules:
  0.0 51.6 jit_solution(13423394898590054217)
XLA Ops:
  0.6 42.8 %features.1 = (f32[32,512]{1,0:T(8,128)}, bf16[16,32,512]{2,1,0:T(8,128)(2,1)}) custom-call(s32[2]{0:T(128)} %len_hbm.1, bf16[512,128]{1,0:T(8,128)(2,1)} %up_hbm.1, bf16[16,128]{1,0:T(8,128)(2,1)} %bitcast.1, bf16[512,512]{1,0:T(8,128)(2,1)} %proj_ref.1, bf16[256,8192]{1,0:T(8,128)(2,1)} %cot_hbm.1, bf16[256,8192]{1,0:T(8,128)(2,1)} %x_hbm.1), custom_call_target="tpu_custom_call" | custom-call | tf_op jit(solution)/shard_map/features/pallas_call | solution.py:237
  43.5 8.1 %gram.1 = (f32[512,8192]{1,0:T(8,128)}, f32[2,8192]{1,0:T(2,128)}) custom-call(bf16[16,32,512]{2,1,0:T(8,128)(2,1)} %get-tuple-element.6.all_ref, f32[32,512]{1,0:T(8,128)} %get-tuple-element.7.feat32_ref), custom_call_target="tpu_custom_call" | custom-call | tf_op jit(solution)/shard_map/gram/pallas_call | solution.py:265

commit v4 on v3

--- a/solution.py
+++ b/solution.py
@@ -63,7 +63,7 @@
     for load in early:
         load.wait()
     part = lax.dot_general(narrow_ref[...], up_ref[...], NT, preferred_element_type=F32)
-    folded[me] = halves(part)
+    folded[me] = part.astype(BF)
     pl.semaphore_wait(barrier, outer + 1)
 
     sent = []
@@ -116,13 +116,12 @@
     send(proj_ref, pin.at[plane], pin_s.at[1, 0], pin_r.at[1, 0], mate_c)
 
     loads[0].wait()
-    sketch = jnp.zeros((2 * rank, x.shape[0]), F32)
+    sketch = jnp.zeros((rank, x.shape[0]), F32)
     for i in range(outer):
         block = jnp.concatenate([folded[i * 4 + j] for j in range(4)], axis=1)
         sketch += lax.dot_general(
             block, cot[:, i * wide:(i + 1) * wide], NT, preferred_element_type=F32
         )
-    sketch = sketch[:rank] + sketch[rank:]
     tok = lax.broadcasted_iota(jnp.int32, (rank, seq), 1)
     mixers = [
         halves(jnp.where(tok < len_ref[e], sketch[:, e * seq:(e + 1) * seq], 0.0))
@@ -248,7 +247,7 @@
             pltpu.VMEM((rank, up.shape[1]), BF),
             pltpu.VMEM((tokens, width), BF),
             pltpu.VMEM((tokens, width), BF),
-            pltpu.VMEM((devices, 2 * rank, depth), BF),
+            pltpu.VMEM((devices, rank, depth), BF),
             pltpu.VMEM((4, depth, kd), BF),
             pltpu.VMEM((outer, rows, 4 * depth), BF),
             pltpu.VMEM((outer, rows, 4 * depth), BF),

time: 51.8 us -> 50.3 us (0.971)
  Pallas kernels: 51 us -> 49.6 us
    pallas_call x1, Pallas kernels: 42.8 us -> 41.4 us  [on_device(): pl.pallas_call(functools.partial(features_kernel, outer), out_shape=(jax....]
where the time goes in v4:
time: 50.3 us; the launch traced here: 50.2 us
  Pallas kernels  49.6 us (99%)
  between operations  0.64 us (1%)
    pallas_call x1, Pallas kernels, on_device(): pl.pallas_call(functools.partial(features_kernel, outer), out_shape=(jax....  41.4 us
    pallas_call x1, Pallas kernels, on_device(): pl.pallas_call(functools.partial(gram_kernel, ex), out_shape=(jax.ShapeDt...  8.14 us

profile of v4, /device:TPU:0, one launch (start us, length us, event | category | flops | bytes accessed | tf_op | source)
XLA Modules:
  0.0 50.2 jit_solution(3866798180455058673)
XLA Ops:
  0.6 41.4 %features.1 = (f32[32,512]{1,0:T(8,128)}, bf16[16,32,512]{2,1,0:T(8,128)(2,1)}) custom-call(s32[2]{0:T(128)} %len_hbm.1, bf16[512,128]{1,0:T(8,128)(2,1)} %up_hbm.1, bf16[16,128]{1,0:T(8,128)(2,1)} %bitcast.1, bf16[512,512]{1,0:T(8,128)(2,1)} %proj_ref.1, bf16[256,8192]{1,0:T(8,128)(2,1)} %cot_hbm.1, bf16[256,8192]{1,0:T(8,128)(2,1)} %x_hbm.1), custom_call_target="tpu_custom_call" | custom-call | tf_op jit(solution)/shard_map/features/pallas_call | solution.py:236
  42.1 8.1 %gram.1 = (f32[512,8192]{1,0:T(8,128)}, f32[2,8192]{1,0:T(2,128)}) custom-call(bf16[16,32,512]{2,1,0:T(8,128)(2,1)} %get-tuple-element.6.all_ref, f32[32,512]{1,0:T(8,128)} %get-tuple-element.7.feat32_ref), custom_call_target="tpu_custom_call" | custom-call | tf_op jit(solution)/shard_map/gram/pallas_call | solution.py:264
